TPU v7x, 32 devices: a whole 2x2x4 slice. The times are simulated.
32 devices in a mesh: ctx: 8 (over y, x, core), tp: 4 (over z).
Axes of the slice: x: 2, y: 2, z: 4, core: 2. Of those that a mesh axis runs over, the one named last changes fastest.
Arguments:
- queries: bfloat16 [1536, 1024], P('ctx', 'tp'), may hold values from -6 to 6
- key_proj: bfloat16 [1536, 1024], P('ctx', 'tp'), may hold values from -6 to 6
- value_proj: bfloat16 [1536, 1024], P('ctx', 'tp'), may hold values from -6 to 6
- filters: float32 [1024, 128], P('tp'), may hold values from -0.5 to 0.5
- offsets: int32 [1536], P('ctx'), may hold values from 0 to 767, as said below
- out_weight: bfloat16 [4096, 1024], P(None, 'tp'), may hold values from -0.1875 to 0.1875
- out_grads: bfloat16 [1536, 4096], P(('ctx', 'tp')), may hold values from -6 to 6
Outputs:
- grad_queries: bfloat16 [1536, 1024], P('ctx', 'tp')
- grad_keys: bfloat16 [1536, 1024], P('ctx', 'tp')
- grad_values: bfloat16 [1536, 1024], P('ctx', 'tp')
- grad_filters: float32 [1024, 128], P('tp')
- grad_weight: float32 [4096, 1024], P('ctx', 'tp')
Inputs may be any that keep to these rules, and one draw needn't show every extreme that they name: offsets counts up by one along each document of the packed sequence and is 0 at a document's first token (always at token 0); a document holds 1 to 768 tokens, and some document holds exactly 768.
All inputs are finite; a program needn't handle non-finite values.
Results may differ from a plain program's by a relative error of at most 0.0051.
Values may be sent and summed in bfloat16 or wider, within the bound.
A program may use at most 64 MiB of HBM per device.

v0:
```python
import jax
import jax.numpy as jnp
from jax import lax
from jax.sharding import PartitionSpec as P


def shifted(value, axis, steps):
    count = lax.axis_size(axis)
    leading, last = (max(0, -steps), min(count, count - steps))
    return lax.ppermute(value, axis, [(source, source + steps) for source in range(leading, last)])


def rounded(values):
    return lax.optimization_barrier(values.astype(jnp.bfloat16))


def block_width():
    return 8


def tap_sum(filters, window_rows, window_cap, out_rows):
    tap_count = filters.shape[1]
    width = block_width()

    def tap_block_step(block_index, running):
        base = block_index * width
        for inner in range(width):
            lag_index = base + inner
            window = lax.dynamic_slice_in_dim(window_rows, lag_index, out_rows, 0)
            cap_rows = lax.dynamic_slice_in_dim(window_cap, lag_index, out_rows, 0)
            coeff = lax.dynamic_slice_in_dim(filters, lag_index, 1, 1)[:, 0]
            running = running + coeff * window * (cap_rows >= lag_index)[:, None]
        return running

    start = jnp.zeros((out_rows, filters.shape[0]), jnp.float32)
    return lax.fori_loop(0, tap_count // width, tap_block_step, start)


def trailing_sum(filters, extended, capped, out_rows):
    tap_count = filters.shape[1]
    rim_rows = tap_count - 1
    width = block_width()

    def trailing_block_step(block_index, running):
        base = block_index * width
        for inner in range(width):
            lag_index = base + inner
            window = lax.dynamic_slice_in_dim(extended, rim_rows - lag_index, out_rows, 0)
            coeff = lax.dynamic_slice_in_dim(filters, lag_index, 1, 1)[:, 0]
            running = running + coeff * window * (capped >= lag_index)[:, None]
        return running

    start = jnp.zeros((out_rows, filters.shape[0]), jnp.float32)
    return lax.fori_loop(0, tap_count // width, trailing_block_step, start)


def filter_columns(filters, extended, capped, grads_wide, out_rows):
    tap_count = filters.shape[1]
    rim_rows = tap_count - 1
    width = block_width()

    def filter_block_step(block_index, running):
        base = block_index * width
        pieces = []
        for inner in range(width):
            lag_index = base + inner
            window = lax.dynamic_slice_in_dim(extended, rim_rows - lag_index, out_rows, 0)
            pieces.append(jnp.sum(grads_wide * window * (capped >= lag_index)[:, None], axis=0))
        block = jnp.stack(pieces, axis=1)
        return lax.dynamic_update_slice_in_dim(running, block, base, 1)

    start = jnp.zeros((filters.shape[0], tap_count), jnp.float32)
    return lax.fori_loop(0, tap_count // width, filter_block_step, start)


def body(queries, key_proj, value_proj, filters, offsets, out_weight, out_grads):
    slab_rows = queries.shape[0]
    channel_count = queries.shape[1]
    tap_count = filters.shape[1]
    rim_rows = tap_count - 1
    grad_scale = float(lax.axis_size("ctx") * slab_rows) ** (-0.5)
    keys_wide = key_proj.astype(jnp.float32)
    values_wide = value_proj.astype(jnp.float32)
    queries_wide = queries.astype(jnp.float32)
    product = rounded(keys_wide * values_wide)
    capped = jnp.minimum(offsets, rim_rows)
    earlier = shifted(product[slab_rows - rim_rows :], "ctx", 1)
    extended = jnp.concatenate([earlier, product], axis=0).astype(jnp.float32)
    filtered = trailing_sum(filters, extended, capped, slab_rows)
    mixed_rows = rounded(queries_wide * filtered)
    slab_piece = lax.all_gather(out_grads, "tp", axis=0, tiled=True)
    grad_block = jnp.dot(slab_piece, out_weight, preferred_element_type=jnp.float32)
    collected = slab_piece
    grad_mixed, collected = (grad_block, collected)
    partial_term = lax.dot_general(
        collected, mixed_rows, (((0,), (0,)), ((), ())), preferred_element_type=jnp.float32
    )
    weight_total = lax.psum_scatter(partial_term, "ctx", scatter_dimension=0, tiled=True)
    grad_weight = weight_total * grad_scale
    grad_filtered = rounded(grad_mixed * queries_wide)
    grad_queries = (grad_mixed * filtered).astype(jnp.bfloat16)
    filtered_wide = grad_filtered.astype(jnp.float32)
    continuing = (offsets[:rim_rows] > jnp.arange(rim_rows, dtype=jnp.int32))[:, None]
    lead_rows = jnp.where(
        continuing, grad_filtered[:rim_rows], jnp.zeros_like(grad_filtered[:rim_rows])
    )
    from_next = shifted(lead_rows, "ctx", -1)
    padded = jnp.concatenate([filtered_wide, from_next.astype(jnp.float32)], axis=0)
    tail_cap = jnp.minimum(
        jnp.arange(rim_rows, dtype=jnp.int32) + 1 + offsets[slab_rows - 1], rim_rows
    )
    padded_cap = jnp.concatenate([capped, tail_cap], axis=0)
    grad_product = tap_sum(filters, padded, padded_cap, slab_rows)
    filter_term = filter_columns(filters, extended, capped, filtered_wide, slab_rows)
    filter_flat = filter_term.reshape(channel_count * tap_count)
    filter_part = lax.psum_scatter(filter_flat, "ctx", scatter_dimension=0, tiled=True) * grad_scale
    filter_whole = lax.all_gather(filter_part, "ctx", axis=0, tiled=True)
    grad_filters = filter_whole.reshape(channel_count, tap_count)
    grad_keys = (grad_product * values_wide).astype(jnp.bfloat16)
    grad_values = (grad_product * keys_wide).astype(jnp.bfloat16)
    return (grad_queries, grad_keys, grad_values, grad_filters, grad_weight)


def solution(mesh):
    in_specs = (
        P("ctx", "tp"),
        P("ctx", "tp"),
        P("ctx", "tp"),
        P("tp", None),
        P("ctx"),
        P(None, "tp"),
        P(("ctx", "tp"), None),
    )
    out_specs = (P("ctx", "tp"), P("ctx", "tp"), P("ctx", "tp"), P("tp", None), P("ctx", "tp"))
    return jax.shard_map(body, mesh=mesh, in_specs=in_specs, out_specs=out_specs, check_vma=False)
```

profile of v0, /device:TPU:0, one launch (start us, length us, event | category | flops | bytes accessed | tf_op | source)
XLA Modules:
  0.0 178.7 jit_solution(9655908643145285103)
XLA Ops:
  7.2 0.7 all-gather.2.cloned.1.call-update
  8.0 1.0 fusion.15
  9.0 2.4 %collective-permute-start = (bf16[127,256]{1,0:T(8,128)(2,1)S(1)}, bf16[127,256]{1,0:T(8,128)(2,1)S(1)}, u32[]{:S(2)}, u32[]{:S(2)}) collective-permute-start(bf16[127,256]{1,0:T(8,128)(2,1)S(1)} %slice.16), channel_id=1, source_target_pairs={{0,4},{4,8},{8,12},{12,16},{16,20},{20,24},{24,28},{1,5},{5,9},{9,... | collective-permute-start | bytes 195080 | tf_op jit(solution)/shard_map/ppermute | solution.py:10
  11.3 1.3 slice.15
  12.6 0.7 iota_compare_fusion
  13.3 0.7 broadcast_minimum_fusion
  14.0 0.6 add_minimum_fusion
  14.6 1.0 copy.20
  15.6 1.2 dynamic-slice
  17.6 8.4 %while.50 = (s32[]{:T(128)}, f32[192,256]{1,0:T(8,128)S(1)}, f32[256,128]{0,1:T(8,128)S(1)}, f32[319,256]{1,0:T(8,128)S(1)}, s32[192]{0:T(256)S(1)}, /*index=5*/...) while((s32[]{:T(128)}, f32[192,256]{1,0:T(8,128)S(1)}, ...), condition=%wide.region_1.0_spmd.clone, body=%wide.region_0.0_spmd.clone.sunk | while | flops 1231939 | bytes 2004775 | solution.py:54
  26.1 23.3 %all-gather.2.cloned.1.call-done = bf16[192,4096]{1,0:T(8,128)(2,1)} async-done(((bf16[48,4096]{1,0:T(8,128)(2,1)}), bf16[192,4096]{1,0:T(8,128)(2,1)}) %all-gather.2.cloned.1.call-update) | async-done | bytes 1572880 | tf_op jit(solution)/shard_map/all_gather | solution.py:91
  49.4 2.0 %fusion.19 = f32[192,256]{1,0:T(8,128)S(1)} fusion(bf16[192,4096]{1,0:T(8,128)(2,1)} %all-gather.2.cloned.1.call-done, bf16[4096,256]{1,0:T(8,128)(2,1)S(1)} %copy-done), kind=kOutput, calls=%fused_computation.86 | convolution fusion | flops 402653184 | bytes 3866624 | tf_op jit(solution)/shard_map/dot_general | solution.py:92
  51.5 0.7 fusion.18
  52.3 1.3 collective-permute-start.1
  53.6 7.8 %while.49 = (s32[]{:T(128)}, f32[256,128]{0,1:T(8,128)S(1)}, f32[319,256]{1,0:T(8,128)S(1)}, f32[192,256]{1,0:T(8,128)S(1)}, s32[192]{0:T(256)S(1)}, /*index=5*/...) while((s32[]{:T(128)}, f32[256,128]{0,1:T(8,128)S(1)}, ...), condition=%wide.region_13.0_spmd, body=%wide.region_4.13_spmd.sunk | while | flops 1180717 | bytes 1824211 | solution.py:73
  61.4 0.8 copy.22
  62.2 4.1 %convolution_bitcast_fusion = f32[4096,256]{0,1:T(8,128)} fusion(bf16[192,256]{1,0:T(8,128)(2,1)S(1)} %get-tuple-element.646, bf16[192,4096]{1,0:T(8,128)(2,1)} %all-gather.2.cloned.1.call-done), kind=kOutput, calls=%fused_computation.65 | convolution fusion | flops 402653184 | bytes 5865472 | tf_op jit(solution)/shard_map/dot_general | solution.py:95
  66.4 9.5 %while.51 = (s32[]{:T(128)}, f32[192,256]{1,0:T(8,128)S(1)}, f32[256,128]{0,1:T(8,128)S(1)}, f32[319,256]{1,0:T(8,128)S(1)}, s32[319]{0:T(512)S(1)}, /*index=5*/...) while((s32[]{:T(128)}, f32[192,256]{1,0:T(8,128)S(1)}, ...), condition=%wide.region_3.4_spmd.clone, body=%wide.region_2.0_spmd.clone.sunk | while | flops 1231923 | bytes 2010063 | solution.py:36
  66.7 0.4 fusion.27
  67.8 0.4 fusion.27
  69.0 0.4 fusion.27
  70.2 0.4 fusion.27
  73.8 0.4 fusion.27
  74.9 0.4 fusion.27
  75.9 0.7 fusion.14
  76.7 38.2 %all-reduce.3.cloned.1.call-done = f32[32768]{0:T(1024)} async-done(((f32[32768]{0:T(1024)}), f32[32768]{0:T(1024)}) %all-reduce.3.cloned.1.call-update) | async-done | bytes 131088
  114.9 0.7 dynamic-slice_multiply_fusion
  115.6 8.5 %all_gather.7 = f32[32768]{0:T(1024)S(1)} all-gather(f32[4096]{0:T(1024)S(1)} %dynamic-slice_multiply_fusion), channel_id=1, replica_groups=mesh['ctx'=8,'tp'=4] {'ctx'}, dimensions={0}, use_global_device_ids=true | all-gather | bytes 147456 | tf_op jit(solution)/shard_map/all_gather | solution.py:117
  124.1 45.3 %reduce-scatter.2.cloned.1.call-done = f32[512,256]{0,1:T(8,128)} async-done(((f32[4096,256]{0,1:T(8,128)}), f32[512,256]{0,1:T(8,128)}) %reduce-scatter.2.cloned.1.call-update) | async-done | bytes 524304 | tf_op jit(solution)/shard_map/reduce_scatter | solution.py:98
  169.4 1.1 broadcast_multiply_fusion
  170.5 1.0 copy.23
  171.5 0.7 copy.45
  (179 shorter events, 19.1 us)
Async XLA Ops:
  7.2 42.3 %copy-start = (bf16[4096,256]{1,0:T(8,128)(2,1)S(1)}, bf16[4096,256]{1,0:T(8,128)(2,1)}, u32[]{:S(2)}) copy-start(bf16[4096,256]{1,0:T(8,128)(2,1)} %param.18) | copy-start | bytes 6291460
  7.2 42.3 %all-gather.2.cloned.1.call-start = ((), (), s32[]{:S(2)}) async-start(), calls=%async_computation.1 | async-start | bytes 1966080 | tf_op jit(solution)/shard_map/all_gather | solution.py:91
  7.9 107.0 %all-reduce.3.cloned.1.call-start = ((), (), s32[]{:S(2)}) async-start(), calls=%async_computation.3 | async-start | bytes 262144
  9.0 8.7 %collective-permute-start = (bf16[127,256]{1,0:T(8,128)(2,1)S(1)}, bf16[127,256]{1,0:T(8,128)(2,1)S(1)}, u32[]{:S(2)}, u32[]{:S(2)}) collective-permute-start(bf16[127,256]{1,0:T(8,128)(2,1)S(1)} %slice.16), channel_id=1, source_target_pairs={{0,4},{4,8},{8,12},{12,16},{16,20},{20,24},{24,28},{1,5},{5,9},{9,... | collective-permute-start | bytes 195080 | tf_op jit(solution)/shard_map/ppermute | solution.py:10
  26.1 25.3 %copy-start.3 = (bf16[192,256]{1,0:T(8,128)(2,1)S(1)}, bf16[192,256]{1,0:T(8,128)(2,1)}, u32[]{:S(2)}) copy-start(bf16[192,256]{1,0:T(8,128)(2,1)} %param.13) | copy-start | bytes 294916
  52.3 14.1 %collective-permute-start.1 = (bf16[127,256]{1,0:T(8,128)(2,1)S(1)}, bf16[127,256]{1,0:T(8,128)(2,1)S(1)}, u32[]{:S(2)}, u32[]{:S(2)}) collective-permute-start(bf16[127,256]{1,0:T(8,128)(2,1)S(1)} %slice_select_fusion), channel_id=1, source_target_pairs={{4,0},{8,4},{12,8},{16,12},{20,16},{24,20},{28,24},{5,1},{9,5},{13... | collective-permute-start | bytes 195080 | tf_op jit(solution)/shard_map/ppermute | solution.py:10
  62.2 107.2 %reduce-scatter.2.cloned.1.call-start = ((), (), s32[]{:S(2)}) async-start(), calls=%async_computation.2 | async-start | bytes 4718592 | tf_op jit(solution)/shard_map/reduce_scatter | solution.py:98
  66.4 9.5 %copy-start.1 = (bf16[192,256]{1,0:T(8,128)(2,1)S(1)}, bf16[192,256]{1,0:T(8,128)(2,1)}, u32[]{:S(2)}) copy-start(bf16[192,256]{1,0:T(8,128)(2,1)} %param.15) | copy-start | bytes 294916
  66.4 9.5 %copy-start.2 = (bf16[192,256]{1,0:T(8,128)(2,1)S(1)}, bf16[192,256]{1,0:T(8,128)(2,1)}, u32[]{:S(2)}) copy-start(bf16[192,256]{1,0:T(8,128)(2,1)} %param.14) | copy-start | bytes 294916
Sparse Core Ops, SparseCore 0:
  9.6 39.8 all-gather.1
  62.3 52.5 all-reduce.2
  118.6 50.7 reduce-scatter.1
where the time goes:
time: 179 us
  waiting for transfers between devices  108 us (60%)
  other arithmetic  25.7 us (14%)
  between operations  14.6 us (8%)
  blocking collectives  8.53 us (5%)
  local copies, waits for them, and re-layouts  7.59 us (4%)
  matrix products  6.05 us (3%)
  loops' own time  4.85 us (3%)
  starting transfers between devices  3.77 us (2%)
    reduce_scatter x1, waiting for transfers between devices, body(): lax.psum_scatter(partial_term, 'ctx', scatter_dimension=0, tiled=True)  45.3 us
    unnamed x4, waiting for transfers between devices  39 us
    all_gather x1, waiting for transfers between devices, body(): slab_piece = lax.all_gather(out_grads, 'tp', axis=0, tiled=True)  23.3 us
    all_gather x1, blocking collectives, body(): filter_whole = lax.all_gather(filter_part, 'ctx', axis=0, tiled=True)  8.53 us
    add x16, other arithmetic, trailing_block_step(): running = running + coeff * window * (capped >= lag_index)[:, None]  5.83 us
    add x16, other arithmetic, tap_block_step(): running = running + coeff * window * (cap_rows >= lag_index)[:, None]  5.82 us
    reduce_sum x16, other arithmetic, filter_block_step(): jnp.sum(grads_wide * window * (capped >= lag_index)[:, None], axis=0)  5.77 us
    dot_general x1, matrix products, body(): lax.dot_general(collected, mixed_rows, (((0,), (0,)), ((), ())), preferre...  4.07 us
  transfers between devices with their start and end apart: 5, of which 3 were waited for; matrix products, arithmetic and copies ran while one was open for 19% of the time, Pallas kernels for 0%

commit v1 on v0

v1 whole, which is shorter than its diff:
```python
import functools

import jax
import jax.numpy as jnp
from jax import lax
from jax.experimental import pallas as pl
from jax.experimental.pallas import tpu as pltpu
from jax.sharding import PartitionSpec as P

MESH = pl.DeviceIdType.MESH
F32 = jnp.float32
BF16 = jnp.bfloat16
LANES = 128
GROUP = 64
WIDTH = 8


def kernel(
    ctx_n, tp_n,
    q_ref, k_ref, v_ref, f_ref, off_ref, w_hbm, og_ref,
    gq_ref, gk_ref, gv_ref, gf_ref, gw_ref,
    wbuf, gbuf, mixed, gm, filt, ext, gext, ft, capb, remb,
    psend, precv, hsend, hrecv, pbuf, xsend, xrecv, xown, rsend, rrecv,
    fg, frecv, fsum,
    w_sem, gs_sem, gr_sem, ps_sem, pr_sem, hs_sem, hr_sem,
    xs_sem, xr_sem, rs_sem, rr_sem, fs_sem, fr_sem, as_sem, ar_sem,
):
    i = lax.axis_index("ctx")
    r = lax.axis_index("tp")
    slab, chans = q_ref.shape
    taps = f_ref.shape[1]
    rows, features = og_ref.shape
    m = ctx_n // 2
    chunk = features // m
    oblk = features // ctx_n
    halves = chans // LANES
    share = taps // ctx_n
    core = lax.rem(i, 2)
    chip = lax.div(i, 2)
    sibling = i + 1 - 2 * core

    barrier = pltpu.get_barrier_semaphore()

    def greet(p, c):
        pl.semaphore_signal(barrier, inc=1, device_id={"ctx": lax.rem(i + p, ctx_n), "tp": r}, device_id_type=MESH)
        return c

    lax.fori_loop(1, ctx_n, greet, 0)

    @pl.when(r > 0)
    def _():
        pl.semaphore_signal(barrier, inc=1, device_id={"ctx": i, "tp": r - 1}, device_id_type=MESH)

    @pl.when(r < tp_n - 1)
    def _():
        pl.semaphore_signal(barrier, inc=1, device_id={"ctx": i, "tp": r + 1}, device_id_type=MESH)

    w_copy = pltpu.make_async_copy(w_hbm, wbuf, w_sem)
    w_copy.start()

    def target(step):
        off = m - 1 - step
        high = lax.rem(lax.div(chip, 2) + lax.div(off, 2), m // 2)
        low = lax.rem(lax.rem(chip, 2) + lax.rem(off, 2), 2)
        return 2 * high + low

    own_rows = pl.ds(pl.multiple_of(r * rows, 16), rows)

    def place(step, c):
        col = pl.multiple_of(target(step) * chunk, 128)
        gbuf[step, own_rows, :] = og_ref[:, pl.ds(col, chunk)]
        return c

    lax.fori_loop(0, m, place, 0)

    product = (k_ref[...].astype(F32) * v_ref[...].astype(F32)).astype(BF16)
    psend[...] = product[slab - taps:, :]
    for h in range(halves):
        ext[h, taps:, :] = product[:, h * LANES:(h + 1) * LANES].astype(F32)
    for h in range(halves):
        ft[h] = f_ref[h * LANES:(h + 1) * LANES, :].T

    lane_tok = lax.broadcasted_iota(jnp.int32, (slab, slab), 1)
    row_tok = lax.broadcasted_iota(jnp.int32, (slab, slab), 0)
    offs = jnp.broadcast_to(off_ref[...], (slab, slab))
    off_col = jnp.sum(jnp.where(lane_tok == row_tok, offs, 0).astype(F32), axis=1, keepdims=True)
    later = jnp.where((lane_tok > row_tok) & (offs == 0), lane_tok - row_tok - 1, taps - 1)
    rem_col = jnp.min(later.astype(F32), axis=1, keepdims=True)
    capb[...] = jnp.broadcast_to(off_col, (slab, LANES)).astype(jnp.int32)
    remb[...] = jnp.broadcast_to(jnp.minimum(rem_col, taps - 1), (slab, LANES)).astype(jnp.int32)
    gm[...] = jnp.zeros_like(gm)

    nbrs = jnp.where(r > 0, 1, 0) + jnp.where(r < tp_n - 1, 1, 0)
    pl.semaphore_wait(barrier, ctx_n - 1 + nbrs)

    def gather_copy(side, step, dist, source, dest):
        window = gbuf.at[step, pl.ds(pl.multiple_of(source * rows, 16), rows), :]
        return pltpu.make_async_remote_copy(
            src_ref=window, dst_ref=window,
            send_sem=gs_sem.at[side, step, dist], recv_sem=gr_sem.at[side, step, dist],
            device_id={"ctx": i, "tp": dest}, device_id_type=MESH,
        )

    def sends(side, step, dist, act):
        if side == 0:
            cond = (r - dist >= 0) & (r + 1 < tp_n)
            source, dest = r - dist, r + 1
        else:
            cond = (r + dist < tp_n) & (r >= 1)
            source, dest = r + dist, r - 1

        @pl.when(cond)
        def _():
            act(gather_copy(side, step, dist, source, dest))

    def arrives(side, step, dist):
        if side == 0:
            cond, source = r - 1 - dist >= 0, r - 1 - dist
            dest = r - 1
        else:
            cond, source = r + 1 + dist < tp_n, r + 1 + dist
            dest = r + 1

        @pl.when(cond)
        def _():
            gather_copy(side, step, dist, source, dest).wait_recv()

    def start(c):
        c.start()

    def done(c):
        c.wait_send()

    for step in range(min(2, m)):
        for side in range(2):
            sends(side, step, 0, start)

    p_copy = pltpu.make_async_remote_copy(
        src_ref=psend, dst_ref=precv, send_sem=ps_sem, recv_sem=pr_sem,
        device_id={"ctx": lax.rem(i + 1, ctx_n), "tp": r}, device_id_type=MESH,
    )
    p_copy.start()
    p_copy.wait()
    earlier = jnp.where(i > 0, precv[...].astype(F32), 0.0)
    for h in range(halves):
        ext[h, :taps, :] = earlier[:, h * LANES:(h + 1) * LANES]

    def tap_sum(source, base_row, sign, caps, emit):
        for g in range(slab // GROUP):
            t0 = g * GROUP
            cap = caps[t0:t0 + GROUP, :]

            def block(b, acc):
                acc = list(acc)
                for s in range(WIDTH):
                    j = b * WIDTH + s
                    keep = cap >= j
                    for h in range(halves):
                        window = source[h, pl.ds(base_row + t0 + sign * j, GROUP), :]
                        coeff = ft[h, pl.ds(j, 1), :]
                        acc[h] = acc[h] + jnp.where(keep, window * coeff, 0.0)
                return tuple(acc)

            zero = tuple(jnp.zeros((GROUP, LANES), F32) for _ in range(halves))
            acc = lax.fori_loop(0, taps // WIDTH, block, zero)
            for h in range(halves):
                emit(t0, h, acc[h])

    def emit_forward(t0, h, value):
        span, cols = slice(t0, t0 + GROUP), slice(h * LANES, (h + 1) * LANES)
        filt[span, cols] = value
        mixed[span, cols] = (q_ref[span, cols].astype(F32) * value).astype(BF16)

    tap_sum(ext, taps, -1, capb, emit_forward)
    w_copy.wait()

    def x_copy(step):
        return pltpu.make_async_remote_copy(
            src_ref=xsend.at[step], dst_ref=xrecv.at[step],
            send_sem=xs_sem.at[step], recv_sem=xr_sem.at[step],
            device_id={"ctx": sibling, "tp": r}, device_id_type=MESH,
        )

    def r_copy(step):
        return pltpu.make_async_remote_copy(
            src_ref=rsend.at[step], dst_ref=rrecv.at[step],
            send_sem=rs_sem.at[step], recv_sem=rr_sem.at[step],
            device_id={"ctx": 2 * target(step) + core, "tp": r}, device_id_type=MESH,
        )

    def forward_pair(step):
        x_copy(step).wait_recv()
        rsend[step] = (xown[step] + xrecv[step].astype(F32)).astype(BF16)
        r_copy(step).start()

    def main(step, c):
        @pl.when(step + 2 < m)
        def _():
            for side in range(2):
                sends(side, step + 2, 0, start)

        for dist in range(tp_n - 1):
            for side in range(2):
                arrives(side, step, dist)
                if dist + 1 < tp_n - 1:
                    sends(side, step, dist + 1, start)
        block = gbuf[step]
        pbuf[...] = lax.dot_general(block, mixed[...], (((0,), (0,)), ((), ())), preferred_element_type=F32)
        xsend[step] = pbuf[pl.ds(pl.multiple_of((1 - core) * oblk, 16), oblk), :].astype(BF16)
        x_copy(step).start()
        xown[step] = pbuf[pl.ds(pl.multiple_of(core * oblk, 16), oblk), :]
        span = pl.ds(pl.multiple_of(target(step) * chunk, 128), chunk)
        gm[...] += jnp.dot(block, wbuf[span, :], preferred_element_type=F32)

        @pl.when(step > 0)
        def _():
            forward_pair(step - 1)

        return c

    lax.fori_loop(0, m, main, 0)

    q_wide = q_ref[...].astype(F32)
    grad_mixed = gm[...]
    grad_filtered = (grad_mixed * q_wide).astype(BF16)
    wide = grad_filtered.astype(F32)
    lead_tok = lax.broadcasted_iota(jnp.int32, (taps, LANES), 0)
    for h in range(halves):
        part = wide[:, h * LANES:(h + 1) * LANES]
        gext[h, :slab, :] = part
        lead = jnp.where(capb[:taps, :] > lead_tok, part[:taps], 0.0)
        hsend[:, h * LANES:(h + 1) * LANES] = lead.astype(BF16)
    h_copy = pltpu.make_async_remote_copy(
        src_ref=hsend, dst_ref=hrecv, send_sem=hs_sem, recv_sem=hr_sem,
        device_id={"ctx": lax.rem(i + ctx_n - 1, ctx_n), "tp": r}, device_id_type=MESH,
    )
    h_copy.start()
    gq_ref[...] = (grad_mixed * filt[...]).astype(BF16)

    def tap_columns(b, c):
        for s in range(WIDTH):
            j = b * WIDTH + s
            total = [jnp.zeros((8, LANES), F32) for _ in range(halves)]
            for g in range(slab // GROUP):
                t0 = g * GROUP
                keep = capb[t0:t0 + GROUP, :] >= j
                for h in range(halves):
                    window = ext[h, pl.ds(taps + t0 - j, GROUP), :]
                    term = jnp.where(keep, window * gext[h, t0:t0 + GROUP, :], 0.0)
                    total[h] = total[h] + jnp.sum(term.reshape(GROUP // 8, 8, LANES), axis=0)
            for h in range(halves):
                fg[lax.div(j, share), h, pl.ds(lax.rem(j, share), 1), :] = jnp.sum(total[h], axis=0, keepdims=True)
        return c

    lax.fori_loop(0, taps // WIDTH, tap_columns, 0)

    def f_copy(p):
        peer = lax.rem(i + p, ctx_n)
        return pltpu.make_async_remote_copy(
            src_ref=fg.at[peer], dst_ref=frecv.at[p], send_sem=fs_sem.at[p], recv_sem=fr_sem.at[p],
            device_id={"ctx": peer, "tp": r}, device_id_type=MESH,
        )

    def a_copy(p):
        return pltpu.make_async_remote_copy(
            src_ref=fsum, dst_ref=gf_ref.at[i], send_sem=as_sem.at[p], recv_sem=ar_sem.at[p],
            device_id={"ctx": lax.rem(i + p, ctx_n), "tp": r}, device_id_type=MESH,
        )

    def a_arrival(p):
        source = lax.rem(i + ctx_n - p, ctx_n)
        return pltpu.make_async_remote_copy(
            src_ref=fsum, dst_ref=gf_ref.at[source], send_sem=as_sem.at[p], recv_sem=ar_sem.at[p],
            device_id={"ctx": source, "tp": r}, device_id_type=MESH,
        )

    def over_peers(act):
        def one(p, c):
            act(p)
            return c

        lax.fori_loop(1, ctx_n, one, 0)

    over_peers(lambda p: f_copy(p).start())

    h_copy.wait()
    follow = jnp.where(i < ctx_n - 1, hrecv[...].astype(F32), 0.0)
    for h in range(halves):
        gext[h, slab:, :] = follow[:, h * LANES:(h + 1) * LANES]

    def emit_backward(t0, h, value):
        span, cols = slice(t0, t0 + GROUP), slice(h * LANES, (h + 1) * LANES)
        gk_ref[span, cols] = (value * v_ref[span, cols].astype(F32)).astype(BF16)
        gv_ref[span, cols] = (value * k_ref[span, cols].astype(F32)).astype(BF16)

    over_peers(lambda p: f_copy(p).wait())
    frecv[0] = fg[i]
    fsum[...] = jnp.sum(frecv[...], axis=0)
    gf_ref[i] = fsum[...]
    over_peers(lambda p: a_copy(p).start())

    tap_sum(gext, 0, 1, remb, emit_backward)

    last = m - 1
    x_copy(last).wait_recv()
    gw_ref[...] = xown[last] + xrecv[last].astype(F32)

    def gather_sum(step, c):
        r_copy(step).wait_recv()
        gw_ref[...] += rrecv[step].astype(F32)
        return c

    lax.fori_loop(0, m - 1, gather_sum, 0)

    def drain(step, c):
        x_copy(step).wait_send()
        for dist in range(tp_n - 1):
            for side in range(2):
                sends(side, step, dist, done)

        @pl.when(step < m - 1)
        def _():
            r_copy(step).wait_send()

        return c

    lax.fori_loop(0, m, drain, 0)
    over_peers(lambda p: a_copy(p).wait_send())
    over_peers(lambda p: a_arrival(p).wait_recv())


def body(ctx_n, tp_n, queries, key_proj, value_proj, filters, offsets, out_weight, out_grads):
    slab, chans = queries.shape
    taps = filters.shape[1]
    rows, features = out_grads.shape
    m = ctx_n // 2
    chunk = features // m
    oblk = features // ctx_n
    halves = chans // LANES
    share = taps // ctx_n
    grad_scale = float(ctx_n * slab) ** (-0.5)
    dma = pltpu.SemaphoreType.DMA
    vmem = pl.BlockSpec(memory_space=pltpu.VMEM)
    sds = jax.ShapeDtypeStruct
    gq, gk, gv, gf, gw = pl.pallas_call(
        functools.partial(kernel, ctx_n, tp_n),
        out_shape=(
            sds((slab, chans), BF16), sds((slab, chans), BF16), sds((slab, chans), BF16),
            sds((ctx_n, halves, share, LANES), F32), sds((oblk, chans), F32),
        ),
        in_specs=[vmem] * 5 + [pl.BlockSpec(memory_space=pl.ANY), vmem],
        out_specs=(vmem,) * 5,
        scratch_shapes=[
            pltpu.VMEM((features, chans), BF16),
            pltpu.VMEM((m, slab, chunk), BF16),
            pltpu.VMEM((slab, chans), BF16),
            pltpu.VMEM((slab, chans), F32),
            pltpu.VMEM((slab, chans), F32),
            pltpu.VMEM((halves, slab + taps, LANES), F32),
            pltpu.VMEM((halves, slab + taps, LANES), F32),
            pltpu.VMEM((halves, taps, LANES), F32),
            pltpu.VMEM((slab, LANES), jnp.int32),
            pltpu.VMEM((slab, LANES), jnp.int32),
            pltpu.VMEM((taps, chans), BF16),
            pltpu.VMEM((taps, chans), BF16),
            pltpu.VMEM((taps, chans), BF16),
            pltpu.VMEM((taps, chans), BF16),
            pltpu.VMEM((chunk, chans), F32),
            pltpu.VMEM((m, oblk, chans), BF16),
            pltpu.VMEM((m, oblk, chans), BF16),
            pltpu.VMEM((m, oblk, chans), F32),
            pltpu.VMEM((m, oblk, chans), BF16),
            pltpu.VMEM((m, oblk, chans), BF16),
            pltpu.VMEM((ctx_n, halves, share, LANES), F32),
            pltpu.VMEM((ctx_n, halves, share, LANES), F32),
            pltpu.VMEM((halves, share, LANES), F32),
            dma, dma((2, m, tp_n)), dma((2, m, tp_n)), dma, dma, dma, dma,
            dma((m,)), dma((m,)), dma((m,)), dma((m,)),
            dma((ctx_n,)), dma((ctx_n,)), dma((ctx_n,)), dma((ctx_n,)),
        ],
        compiler_params=pltpu.CompilerParams(
            collective_id=0, has_side_effects=True, vmem_limit_bytes=48 * 1024 * 1024
        ),
    )(queries, key_proj, value_proj, filters, offsets.reshape(1, slab), out_weight, out_grads)
    grad_filters = jnp.transpose(gf * grad_scale, (1, 3, 0, 2)).reshape(chans, taps)
    return gq, gk, gv, grad_filters, gw * grad_scale


def solution(mesh):
    in_specs = (
        P("ctx", "tp"),
        P("ctx", "tp"),
        P("ctx", "tp"),
        P("tp", None),
        P("ctx"),
        P(None, "tp"),
        P(("ctx", "tp"), None),
    )
    out_specs = (P("ctx", "tp"), P("ctx", "tp"), P("ctx", "tp"), P("tp", None), P("ctx", "tp"))
    step = functools.partial(body, mesh.shape["ctx"], mesh.shape["tp"])
    return jax.shard_map(step, mesh=mesh, in_specs=in_specs, out_specs=out_specs, check_vma=False)
```

time: 179 us -> 59.7 us (0.33)
  waiting for transfers between devices: 108 us -> 0 us
  Pallas kernels: 0 us -> 48.2 us
  other arithmetic: 25.7 us -> 0.86 us
  between operations: 14.6 us -> 0.68 us
  blocking collectives: 8.53 us -> 0 us
  matrix products: 6.05 us -> 0 us
  loops' own time: 4.85 us -> 0 us
  starting transfers between devices: 3.77 us -> 0 us
  local copies, waits for them, and re-layouts: 7.59 us -> 9.59 us
    pallas_call x0 -> x1, Pallas kernels: none -> 48.2 us  [body(): pl.pallas_call(functools.partial(kernel, ctx_n, tp_n), out_shape=(sds((sl...]
    reduce_scatter x1 -> x0, waiting for transfers between devices: 45.3 us -> none  [body(): lax.psum_scatter(partial_term, 'ctx', scatter_dimension=0, tiled=True)]
    unnamed x4 -> x0, waiting for transfers between devices: 39 us -> none
    all_gather x1 -> x0, waiting for transfers between devices: 23.3 us -> none  [body(): slab_piece = lax.all_gather(out_grads, 'tp', axis=0, tiled=True)]
    add x32 -> x0, other arithmetic: 11.6 us -> none  [the longest x16 5.83 us: trailing_block_step(): running = running + coeff * window * (capped >= lag_index)[:, None]]
    all_gather x1 -> x0, blocking collectives: 8.53 us -> none  [body(): filter_whole = lax.all_gather(filter_part, 'ctx', axis=0, tiled=True)]
    dot_general x2 -> x0, matrix products: 6.05 us -> none  [the longest x1 4.07 us: body(): lax.dot_general(collected, mixed_rows, (((0,), (0,)), ((), ())), preferre...]
    reduce_sum x16 -> x0, other arithmetic: 5.77 us -> none  [filter_block_step(): jnp.sum(grads_wide * window * (capped >= lag_index)[:, None], axis=0)]
  transfers between devices with their start and end apart: 5 -> 0, of which waited for: 3 -> 0; matrix products, arithmetic and copies ran while one was open for 19% -> 0% of each run, Pallas kernels for 0% -> 0%
where the time goes in v1:
time: 59.7 us; the launch traced here: 59.4 us
  Pallas kernels  48.2 us (81%)
  local copies, waits for them, and re-layouts  9.59 us (16%)
  other arithmetic  0.86 us (1%)
  between operations  0.68 us (1%)
    pallas_call x1, Pallas kernels, body(): pl.pallas_call(functools.partial(kernel, ctx_n, tp_n), out_shape=(sds((sl...  48.2 us
    unnamed x19, local copies, waits for them, and re-layouts  9.52 us

profile of v1, /device:TPU:0, one launch (start us, length us, event | category | flops | bytes accessed | tf_op | source)
XLA Modules:
  0.0 59.4 jit_solution(9368154825420592023)
XLA Ops:
  0.6 0.0 copy-start
  0.6 1.6 %copy-done = bf16[4096,256]{1,0:T(8,128)(2,1)S(1)} copy-done((bf16[4096,256]{1,0:T(8,128)(2,1)S(1)}, bf16[4096,256]{1,0:T(8,128)(2,1)}, u32[]{:S(2)}) %copy-start) | copy-done | bytes 2097176
  2.2 0.0 copy-start.1
  2.2 1.0 %copy-done.1 = bf16[48,4096]{1,0:T(8,128)(2,1)S(1)} copy-done((bf16[48,4096]{1,0:T(8,128)(2,1)S(1)}, bf16[48,4096]{1,0:T(8,128)(2,1)}, u32[]{:S(2)}) %copy-start.1) | copy-done | bytes 393240
  3.2 0.0 copy-start.2
  3.2 0.9 %copy-done.2 = f32[256,128]{1,0:T(8,128)S(1)} copy-done((f32[256,128]{1,0:T(8,128)S(1)}, f32[256,128]{1,0:T(8,128)}, u32[]{:S(2)}) %copy-start.2) | copy-done | bytes 131096
  4.1 0.0 copy-start.3
  4.1 0.9 %copy-done.3 = bf16[192,256]{1,0:T(8,128)(2,1)S(1)} copy-done((bf16[192,256]{1,0:T(8,128)(2,1)S(1)}, bf16[192,256]{1,0:T(8,128)(2,1)}, u32[]{:S(2)}) %copy-start.3) | copy-done | bytes 98328
  5.0 0.0 copy-start.4
  5.0 0.9 %copy-done.4 = bf16[192,256]{1,0:T(8,128)(2,1)S(1)} copy-done((bf16[192,256]{1,0:T(8,128)(2,1)S(1)}, bf16[192,256]{1,0:T(8,128)(2,1)}, u32[]{:S(2)}) %copy-start.4) | copy-done | bytes 98328
  5.9 0.0 copy-start.5
  5.9 0.9 %copy-done.5 = bf16[192,256]{1,0:T(8,128)(2,1)S(1)} copy-done((bf16[192,256]{1,0:T(8,128)(2,1)S(1)}, bf16[192,256]{1,0:T(8,128)(2,1)}, u32[]{:S(2)}) %copy-start.5) | copy-done | bytes 98328
  6.8 0.0 copy-start.6
  6.8 0.7 %copy-done.6 = s32[192]{0:T(256)S(1)} copy-done((s32[192]{0:T(256)S(1)}, s32[192]{0:T(256)}, u32[]{:S(2)}) %copy-start.6) | copy-done | bytes 792
  7.5 48.2 %shard_map.110 = (bf16[192,256]{1,0:T(8,128)(2,1)S(1)}, bf16[192,256]{1,0:T(8,128)(2,1)S(1)}, bf16[192,256]{1,0:T(8,128)(2,1)S(1)}, f32[8,2,16,128]{3,2,1,0:T(8,128)S(1)}, f32[512,256]{1,0:T(8,128)S(1)}) custom-call(bf16[192,256]{1,0:T(8,128)(2,1)S(1)} %copy-done.3, bf16[192,256]{1,0:T(8,128)(2,1)S(1)} %copy-done.4, bf16[192,256]{1,0:T(8,128)(2,1)S(1)} %copy-done.5, ...), custom_call_target="tpu_custom_call" | custom-call | tf_op jit(solution)/shard_map/pallas_call | solution.py:345
  55.7 0.1 copy.12
  55.8 0.8 %copy.13 = f32[256,128]{1,0:T(8,128)} copy(f32[256,128]{0,1:T(8,128)S(1)} %bitcast.12) | data formatting | bytes 262144
  56.6 0.8 %broadcast_multiply_fusion = f32[512,256]{1,0:T(8,128)} fusion(f32[512,256]{1,0:T(8,128)S(1)} %get-tuple-element.14), kind=kLoop, calls=%fused_computation | loop fusion | flops 131072 | bytes 1048576 | tf_op jit(solution)/shard_map/mul | solution.py:386
  57.4 0.6 %copy.20 = bf16[192,256]{1,0:T(8,128)(2,1)} copy(bf16[192,256]{1,0:T(8,128)(2,1)S(1)} %get-tuple-element.25) | data formatting | bytes 196608
  58.1 0.6 %copy.21 = bf16[192,256]{1,0:T(8,128)(2,1)} copy(bf16[192,256]{1,0:T(8,128)(2,1)S(1)} %get-tuple-element.26) | data formatting | bytes 196608
  58.7 0.6 %copy.22 = bf16[192,256]{1,0:T(8,128)(2,1)} copy(bf16[192,256]{1,0:T(8,128)(2,1)S(1)} %get-tuple-element.27) | data formatting | bytes 196608
  (2 shorter events, 0.0 us)
Async XLA Ops:
  0.6 1.6 %copy-start = (bf16[4096,256]{1,0:T(8,128)(2,1)S(1)}, bf16[4096,256]{1,0:T(8,128)(2,1)}, u32[]{:S(2)}) copy-start(bf16[4096,256]{1,0:T(8,128)(2,1)} %w_hbm.1) | copy-start | bytes 6291460
  2.2 1.0 %copy-start.1 = (bf16[48,4096]{1,0:T(8,128)(2,1)S(1)}, bf16[48,4096]{1,0:T(8,128)(2,1)}, u32[]{:S(2)}) copy-start(bf16[48,4096]{1,0:T(8,128)(2,1)} %og_ref.1) | copy-start | bytes 1179652
  3.2 0.9 %copy-start.2 = (f32[256,128]{1,0:T(8,128)S(1)}, f32[256,128]{1,0:T(8,128)}, u32[]{:S(2)}) copy-start(f32[256,128]{1,0:T(8,128)} %f_ref.1) | copy-start | bytes 393220
  4.1 0.9 %copy-start.3 = (bf16[192,256]{1,0:T(8,128)(2,1)S(1)}, bf16[192,256]{1,0:T(8,128)(2,1)}, u32[]{:S(2)}) copy-start(bf16[192,256]{1,0:T(8,128)(2,1)} %q_ref.1) | copy-start | bytes 294916
  5.0 0.9 %copy-start.4 = (bf16[192,256]{1,0:T(8,128)(2,1)S(1)}, bf16[192,256]{1,0:T(8,128)(2,1)}, u32[]{:S(2)}) copy-start(bf16[192,256]{1,0:T(8,128)(2,1)} %k_ref.1) | copy-start | bytes 294916
  5.9 0.9 %copy-start.5 = (bf16[192,256]{1,0:T(8,128)(2,1)S(1)}, bf16[192,256]{1,0:T(8,128)(2,1)}, u32[]{:S(2)}) copy-start(bf16[192,256]{1,0:T(8,128)(2,1)} %v_ref.1) | copy-start | bytes 294916
  6.8 0.7 %copy-start.6 = (s32[192]{0:T(256)S(1)}, s32[192]{0:T(256)}, u32[]{:S(2)}) copy-start(s32[192]{0:T(256)} %param.11) | copy-start | bytes 2308

commit v2 on v1

--- a/solution.py
+++ b/solution.py
@@ -17,12 +17,12 @@
 
 def kernel(
     ctx_n, tp_n,
-    q_ref, k_ref, v_ref, f_ref, off_ref, w_hbm, og_ref,
+    q_hbm, k_hbm, v_hbm, f_hbm, off_hbm, w_hbm, og_ref,
     gq_ref, gk_ref, gv_ref, gf_ref, gw_ref,
     wbuf, gbuf, mixed, gm, filt, ext, gext, ft, capb, remb,
     psend, precv, hsend, hrecv, pbuf, xsend, xrecv, xown, rsend, rrecv,
-    fg, frecv, fsum,
-    w_sem, gs_sem, gr_sem, ps_sem, pr_sem, hs_sem, hr_sem,
+    fg, frecv, fsum, q_ref, k_ref, v_ref, f_ref, off_ref,
+    in_sem, og_sem, w_sem, gs_sem, gr_sem, ps_sem, pr_sem, hs_sem, hr_sem,
     xs_sem, xr_sem, rs_sem, rr_sem, fs_sem, fr_sem, as_sem, ar_sem,
 ):
     i = lax.axis_index("ctx")
@@ -55,9 +55,6 @@
     def _():
         pl.semaphore_signal(barrier, inc=1, device_id={"ctx": i, "tp": r + 1}, device_id_type=MESH)
 
-    w_copy = pltpu.make_async_copy(w_hbm, wbuf, w_sem)
-    w_copy.start()
-
     def target(step):
         off = m - 1 - step
         high = lax.rem(lax.div(chip, 2) + lax.div(off, 2), m // 2)
@@ -66,17 +63,87 @@
 
     own_rows = pl.ds(pl.multiple_of(r * rows, 16), rows)
 
-    def place(step, c):
-        col = pl.multiple_of(target(step) * chunk, 128)
-        gbuf[step, own_rows, :] = og_ref[:, pl.ds(col, chunk)]
-        return c
-
-    lax.fori_loop(0, m, place, 0)
-
+    def own_columns(step):
+        return og_ref.at[:, pl.ds(pl.multiple_of(target(step) * chunk, 128), chunk)]
+
+    def place(step):
+        return pltpu.make_async_copy(own_columns(step), gbuf.at[step, own_rows, :], og_sem.at[step])
+
+    loads = [
+        pltpu.make_async_copy(source, held, in_sem.at[n])
+        for n, (source, held) in enumerate((
+            (k_hbm, k_ref), (v_hbm, v_ref), (off_hbm, off_ref), (f_hbm, f_ref), (q_hbm, q_ref)
+        ))
+    ]
+    for load in loads:
+        load.start()
+
+    def place_all(step, c):
+        place(step).start()
+        return c
+
+    lax.fori_loop(0, m, place_all, 0)
+    w_copy = pltpu.make_async_copy(w_hbm, wbuf, w_sem)
+    w_copy.start()
+    nbrs = jnp.where(r > 0, 1, 0) + jnp.where(r < tp_n - 1, 1, 0)
+    pl.semaphore_wait(barrier, ctx_n - 1 + nbrs)
+
+    def gather_copy(side, step, dist, source, dest):
+        window = gbuf.at[step, pl.ds(pl.multiple_of(source * rows, 16), rows), :]
+        return pltpu.make_async_remote_copy(
+            src_ref=own_columns(step) if dist == 0 else window, dst_ref=window,
+            send_sem=gs_sem.at[side, step, dist], recv_sem=gr_sem.at[side, step, dist],
+            device_id={"ctx": i, "tp": dest}, device_id_type=MESH,
+        )
+
+    def sends(side, step, dist, act):
+        if side == 0:
+            cond = (r - dist >= 0) & (r + 1 < tp_n)
+            source, dest = r - dist, r + 1
+        else:
+            cond = (r + dist < tp_n) & (r >= 1)
+            source, dest = r + dist, r - 1
+
+        @pl.when(cond)
+        def _():
+            act(gather_copy(side, step, dist, source, dest))
+
+    def arrives(side, step, dist):
+        if side == 0:
+            cond, source = r - 1 - dist >= 0, r - 1 - dist
+            dest = r - 1
+        else:
+            cond, source = r + 1 + dist < tp_n, r + 1 + dist
+            dest = r + 1
+
+        @pl.when(cond)
+        def _():
+            gather_copy(side, step, dist, source, dest).wait_recv()
+
+    def start(c):
+        c.start()
+
+    def done(c):
+        c.wait_send()
+
+    for step in range(min(2, m)):
+        for side in range(2):
+            sends(side, step, 0, start)
+
+
+    loads[0].wait()
+    loads[1].wait()
     product = (k_ref[...].astype(F32) * v_ref[...].astype(F32)).astype(BF16)
     psend[...] = product[slab - taps:, :]
+    p_copy = pltpu.make_async_remote_copy(
+        src_ref=psend, dst_ref=precv, send_sem=ps_sem, recv_sem=pr_sem,
+        device_id={"ctx": lax.rem(i + 1, ctx_n), "tp": r}, device_id_type=MESH,
+    )
+    p_copy.start()
     for h in range(halves):
         ext[h, taps:, :] = product[:, h * LANES:(h + 1) * LANES].astype(F32)
+    loads[2].wait()
+    loads[3].wait()
     for h in range(halves):
         ft[h] = f_ref[h * LANES:(h + 1) * LANES, :].T
 
@@ -90,56 +157,7 @@
     remb[...] = jnp.broadcast_to(jnp.minimum(rem_col, taps - 1), (slab, LANES)).astype(jnp.int32)
     gm[...] = jnp.zeros_like(gm)
 
-    nbrs = jnp.where(r > 0, 1, 0) + jnp.where(r < tp_n - 1, 1, 0)
-    pl.semaphore_wait(barrier, ctx_n - 1 + nbrs)
-
-    def gather_copy(side, step, dist, source, dest):
-        window = gbuf.at[step, pl.ds(pl.multiple_of(source * rows, 16), rows), :]
-        return pltpu.make_async_remote_copy(
-            src_ref=window, dst_ref=window,
-            send_sem=gs_sem.at[side, step, dist], recv_sem=gr_sem.at[side, step, dist],
-            device_id={"ctx": i, "tp": dest}, device_id_type=MESH,
-        )
-
-    def sends(side, step, dist, act):
-        if side == 0:
-            cond = (r - dist >= 0) & (r + 1 < tp_n)
-            source, dest = r - dist, r + 1
-        else:
-            cond = (r + dist < tp_n) & (r >= 1)
-            source, dest = r + dist, r - 1
-
-        @pl.when(cond)
-        def _():
-            act(gather_copy(side, step, dist, source, dest))
-
-    def arrives(side, step, dist):
-        if side == 0:
-            cond, source = r - 1 - dist >= 0, r - 1 - dist
-            dest = r - 1
-        else:
-            cond, source = r + 1 + dist < tp_n, r + 1 + dist
-            dest = r + 1
-
-        @pl.when(cond)
-        def _():
-            gather_copy(side, step, dist, source, dest).wait_recv()
-
-    def start(c):
-        c.start()
-
-    def done(c):
-        c.wait_send()
-
-    for step in range(min(2, m)):
-        for side in range(2):
-            sends(side, step, 0, start)
-
-    p_copy = pltpu.make_async_remote_copy(
-        src_ref=psend, dst_ref=precv, send_sem=ps_sem, recv_sem=pr_sem,
-        device_id={"ctx": lax.rem(i + 1, ctx_n), "tp": r}, device_id_type=MESH,
-    )
-    p_copy.start()
+    loads[4].wait()
     p_copy.wait()
     earlier = jnp.where(i > 0, precv[...].astype(F32), 0.0)
     for h in range(halves):
@@ -199,11 +217,18 @@
             for side in range(2):
                 sends(side, step + 2, 0, start)
 
+        place(step).wait()
         for dist in range(tp_n - 1):
             for side in range(2):
                 arrives(side, step, dist)
                 if dist + 1 < tp_n - 1:
                     sends(side, step, dist + 1, start)
+            if dist == 0:
+
+                @pl.when(step > 0)
+                def _():
+                    forward_pair(step - 1)
+
         block = gbuf[step]
         pbuf[...] = lax.dot_general(block, mixed[...], (((0,), (0,)), ((), ())), preferred_element_type=F32)
         xsend[step] = pbuf[pl.ds(pl.multiple_of((1 - core) * oblk, 16), oblk), :].astype(BF16)
@@ -211,10 +236,6 @@
         xown[step] = pbuf[pl.ds(pl.multiple_of(core * oblk, 16), oblk), :]
         span = pl.ds(pl.multiple_of(target(step) * chunk, 128), chunk)
         gm[...] += jnp.dot(block, wbuf[span, :], preferred_element_type=F32)
-
-        @pl.when(step > 0)
-        def _():
-            forward_pair(step - 1)
 
         return c
 
@@ -327,6 +348,18 @@
     lax.fori_loop(0, m, drain, 0)
     over_peers(lambda p: a_copy(p).wait_send())
     over_peers(lambda p: a_arrival(p).wait_recv())
+
+
+def finish(scale, gq_ref, gk_ref, gv_ref, gf_ref, gw_ref, oq_ref, ok_ref, ov_ref, of_ref, ow_ref, flat):
+    ow_ref[...] = gw_ref[...] * scale
+    oq_ref[...] = gq_ref[...]
+    ok_ref[...] = gk_ref[...]
+    ov_ref[...] = gv_ref[...]
+    parts, halves, share, lanes = gf_ref.shape
+    for h in range(halves):
+        for part in range(parts):
+            flat[part * share:(part + 1) * share, :] = gf_ref[part, h] * scale
+        of_ref[h * lanes:(h + 1) * lanes, :] = flat[...].T
 
 
 def body(ctx_n, tp_n, queries, key_proj, value_proj, filters, offsets, out_weight, out_grads):
@@ -348,7 +381,7 @@
             sds((slab, chans), BF16), sds((slab, chans), BF16), sds((slab, chans), BF16),
             sds((ctx_n, halves, share, LANES), F32), sds((oblk, chans), F32),
         ),
-        in_specs=[vmem] * 5 + [pl.BlockSpec(memory_space=pl.ANY), vmem],
+        in_specs=[pl.BlockSpec(memory_space=pl.ANY)] * 7,
         out_specs=(vmem,) * 5,
         scratch_shapes=[
             pltpu.VMEM((features, chans), BF16),
@@ -374,16 +407,29 @@
             pltpu.VMEM((ctx_n, halves, share, LANES), F32),
             pltpu.VMEM((ctx_n, halves, share, LANES), F32),
             pltpu.VMEM((halves, share, LANES), F32),
-            dma, dma((2, m, tp_n)), dma((2, m, tp_n)), dma, dma, dma, dma,
+            pltpu.VMEM((slab, chans), BF16),
+            pltpu.VMEM((slab, chans), BF16),
+            pltpu.VMEM((slab, chans), BF16),
+            pltpu.VMEM((chans, taps), F32),
+            pltpu.VMEM((1, slab), jnp.int32),
+            dma((5,)), dma((m,)), dma, dma((2, m, tp_n)), dma((2, m, tp_n)), dma, dma, dma, dma,
             dma((m,)), dma((m,)), dma((m,)), dma((m,)),
             dma((ctx_n,)), dma((ctx_n,)), dma((ctx_n,)), dma((ctx_n,)),
         ],
         compiler_params=pltpu.CompilerParams(
-            collective_id=0, has_side_effects=True, vmem_limit_bytes=48 * 1024 * 1024
+            collective_id=0, has_side_effects=True, vmem_limit_bytes=62 * 1024 * 1024
         ),
     )(queries, key_proj, value_proj, filters, offsets.reshape(1, slab), out_weight, out_grads)
-    grad_filters = jnp.transpose(gf * grad_scale, (1, 3, 0, 2)).reshape(chans, taps)
-    return gq, gk, gv, grad_filters, gw * grad_scale
+    return pl.pallas_call(
+        functools.partial(finish, grad_scale),
+        out_shape=(
+            sds((slab, chans), BF16), sds((slab, chans), BF16), sds((slab, chans), BF16),
+            sds((chans, taps), F32), sds((oblk, chans), F32),
+        ),
+        in_specs=[vmem] * 5,
+        out_specs=(vmem,) * 5,
+        scratch_shapes=[pltpu.VMEM((taps, LANES), F32)],
+    )(gq, gk, gv, gf, gw)
 
 
 def solution(mesh):

time: 59.7 us -> 51.7 us (0.87)
  local copies, waits for them, and re-layouts: 9.59 us -> 0 us
  Pallas kernels: 48.2 us -> 50.9 us
  other arithmetic: 0.86 us -> 0 us
    unnamed x19 -> x0, local copies, waits for them, and re-layouts: 9.52 us -> none
    pallas_call x0 -> x1, Pallas kernels: none -> 2.21 us  [body(): pl.pallas_call(functools.partial(finish, grad_scale), out_shape=(sds((sla...]
    mul x1 -> x0, other arithmetic: 0.84 us -> none  [body(): return (gq, gk, gv, grad_filters, gw * grad_scale)]
where the time goes in v2:
time: 51.7 us; the launch traced here: 51.5 us
  Pallas kernels  50.9 us (98%)
  between operations  0.64 us (1%)
    pallas_call x1, Pallas kernels, body(): pl.pallas_call(functools.partial(kernel, ctx_n, tp_n), out_shape=(sds((sl...  48.7 us
    pallas_call x1, Pallas kernels, body(): pl.pallas_call(functools.partial(finish, grad_scale), out_shape=(sds((sla...  2.21 us

profile of v2, /device:TPU:0, one launch (start us, length us, event | category | flops | bytes accessed | tf_op | source)
XLA Modules:
  0.0 51.5 jit_solution(11163003456220496368)
XLA Ops:
  0.6 48.7 %shard_map.110 = (bf16[192,256]{1,0:T(8,128)(2,1)}, bf16[192,256]{1,0:T(8,128)(2,1)}, bf16[192,256]{1,0:T(8,128)(2,1)}, f32[8,2,16,128]{3,2,1,0:T(8,128)}, f32[512,256]{1,0:T(8,128)}) custom-call(bf16[192,256]{1,0:T(8,128)(2,1)} %q_hbm.1, bf16[192,256]{1,0:T(8,128)(2,1)} %k_hbm.1, bf16[192,256]{1,0:T(8,128)(2,1)} %v_hbm.1, f32[256,128]{1,0:T(8,128)} %f_hbm.1, ...), custom_call_target="tpu_custom_call" | custom-call | tf_op jit(solution)/shard_map/pallas_call | solution.py:378
  49.3 2.2 %shard_map.111 = (bf16[192,256]{1,0:T(8,128)(2,1)}, bf16[192,256]{1,0:T(8,128)(2,1)}, bf16[192,256]{1,0:T(8,128)(2,1)}, f32[256,128]{1,0:T(8,128)}, f32[512,256]{1,0:T(8,128)}) custom-call(bf16[192,256]{1,0:T(8,128)(2,1)} %get-tuple-element.10.gq_ref, bf16[192,256]{1,0:T(8,128)(2,1)} %get-tuple-element.11.gk_ref, bf16[192,256]{1,0:T(8,128)(2,1)} %get-tuple-element.12.gv_ref, ...), custom_call_target="tpu_custom_call" | custom-call | tf_op jit(solution)/shard_map/pallas_call | solution.py:423

commit v3 on v2

--- a/solution.py
+++ b/solution.py
@@ -126,7 +126,7 @@
     def done(c):
         c.wait_send()
 
-    for step in range(min(2, m)):
+    for step in range(min(4, m)):
         for side in range(2):
             sends(side, step, 0, start)
 
@@ -212,10 +212,10 @@
         r_copy(step).start()
 
     def main(step, c):
-        @pl.when(step + 2 < m)
+        @pl.when(step + 4 < m)
         def _():
             for side in range(2):
-                sends(side, step + 2, 0, start)
+                sends(side, step + 4, 0, start)
 
         place(step).wait()
         for dist in range(tp_n - 1):

time: 51.7 us -> 52.1 us (level)
  no operation moved by 1% of the time
where the time goes in v3:
time: 52.1 us; the launch traced here: 51.9 us
  Pallas kernels  51.3 us (98%)
  between operations  0.64 us (1%)
    pallas_call x1, Pallas kernels, body(): pl.pallas_call(functools.partial(kernel, ctx_n, tp_n), out_shape=(sds((sl...  49.1 us
    pallas_call x1, Pallas kernels, body(): pl.pallas_call(functools.partial(finish, grad_scale), out_shape=(sds((sla...  2.21 us

profile of v3, /device:TPU:0, one launch (start us, length us, event | category | flops | bytes accessed | tf_op | source)
XLA Modules:
  0.0 51.9 jit_solution(15546396873815022826)
XLA Ops:
  0.6 49.1 %shard_map.110 = (bf16[192,256]{1,0:T(8,128)(2,1)}, bf16[192,256]{1,0:T(8,128)(2,1)}, bf16[192,256]{1,0:T(8,128)(2,1)}, f32[8,2,16,128]{3,2,1,0:T(8,128)}, f32[512,256]{1,0:T(8,128)}) custom-call(bf16[192,256]{1,0:T(8,128)(2,1)} %q_hbm.1, bf16[192,256]{1,0:T(8,128)(2,1)} %k_hbm.1, bf16[192,256]{1,0:T(8,128)(2,1)} %v_hbm.1, f32[256,128]{1,0:T(8,128)} %f_hbm.1, ...), custom_call_target="tpu_custom_call" | custom-call | tf_op jit(solution)/shard_map/pallas_call | solution.py:378
  49.7 2.2 %shard_map.111 = (bf16[192,256]{1,0:T(8,128)(2,1)}, bf16[192,256]{1,0:T(8,128)(2,1)}, bf16[192,256]{1,0:T(8,128)(2,1)}, f32[256,128]{1,0:T(8,128)}, f32[512,256]{1,0:T(8,128)}) custom-call(bf16[192,256]{1,0:T(8,128)(2,1)} %get-tuple-element.10.gq_ref, bf16[192,256]{1,0:T(8,128)(2,1)} %get-tuple-element.11.gk_ref, bf16[192,256]{1,0:T(8,128)(2,1)} %get-tuple-element.12.gv_ref, ...), custom_call_target="tpu_custom_call" | custom-call | tf_op jit(solution)/shard_map/pallas_call | solution.py:423

commit v4 on v2

--- a/solution.py
+++ b/solution.py
@@ -157,12 +157,6 @@
     remb[...] = jnp.broadcast_to(jnp.minimum(rem_col, taps - 1), (slab, LANES)).astype(jnp.int32)
     gm[...] = jnp.zeros_like(gm)
 
-    loads[4].wait()
-    p_copy.wait()
-    earlier = jnp.where(i > 0, precv[...].astype(F32), 0.0)
-    for h in range(halves):
-        ext[h, :taps, :] = earlier[:, h * LANES:(h + 1) * LANES]
-
     def tap_sum(source, base_row, sign, caps, emit):
         for g in range(slab // GROUP):
             t0 = g * GROUP
@@ -189,8 +183,14 @@
         filt[span, cols] = value
         mixed[span, cols] = (q_ref[span, cols].astype(F32) * value).astype(BF16)
 
-    tap_sum(ext, taps, -1, capb, emit_forward)
-    w_copy.wait()
+    def forward_taps():
+        loads[4].wait()
+        p_copy.wait()
+        earlier = jnp.where(i > 0, precv[...].astype(F32), 0.0)
+        for h in range(halves):
+            ext[h, :taps, :] = earlier[:, h * LANES:(h + 1) * LANES]
+        tap_sum(ext, taps, -1, capb, emit_forward)
+        w_copy.wait()
 
     def x_copy(step):
         return pltpu.make_async_remote_copy(
@@ -211,24 +211,14 @@
         rsend[step] = (xown[step] + xrecv[step].astype(F32)).astype(BF16)
         r_copy(step).start()
 
-    def main(step, c):
-        @pl.when(step + 2 < m)
-        def _():
-            for side in range(2):
-                sends(side, step + 2, 0, start)
+    lag = tp_n - 2
+
+    def compute(step):
+        @pl.when(step > 0)
+        def _():
+            forward_pair(step - 1)
 
         place(step).wait()
-        for dist in range(tp_n - 1):
-            for side in range(2):
-                arrives(side, step, dist)
-                if dist + 1 < tp_n - 1:
-                    sends(side, step, dist + 1, start)
-            if dist == 0:
-
-                @pl.when(step > 0)
-                def _():
-                    forward_pair(step - 1)
-
         block = gbuf[step]
         pbuf[...] = lax.dot_general(block, mixed[...], (((0,), (0,)), ((), ())), preferred_element_type=F32)
         xsend[step] = pbuf[pl.ds(pl.multiple_of((1 - core) * oblk, 16), oblk), :].astype(BF16)
@@ -237,9 +227,33 @@
         span = pl.ds(pl.multiple_of(target(step) * chunk, 128), chunk)
         gm[...] += jnp.dot(block, wbuf[span, :], preferred_element_type=F32)
 
-        return c
-
-    lax.fori_loop(0, m, main, 0)
+    def main(turn, c):
+        @pl.when(turn + 2 < m)
+        def _():
+            for side in range(2):
+                sends(side, turn + 2, 0, start)
+
+        for dist in range(tp_n - 1):
+            step = turn - dist
+
+            @pl.when((step >= 0) & (step < m))
+            def _():
+                for side in range(2):
+                    arrives(side, step, dist)
+                    if dist + 1 < tp_n - 1:
+                        sends(side, step, dist + 1, start)
+
+        @pl.when(turn == 0)
+        def _():
+            forward_taps()
+
+        @pl.when(turn >= lag)
+        def _():
+            compute(turn - lag)
+
+        return c
+
+    lax.fori_loop(0, m + lag, main, 0)
 
     q_wide = q_ref[...].astype(F32)
     grad_mixed = gm[...]

time: 51.7 us -> 51 us (0.986)
  Pallas kernels: 50.9 us -> 50.3 us
    pallas_call x1, Pallas kernels: 48.7 us -> 48 us  [body(): pl.pallas_call(functools.partial(kernel, ctx_n, tp_n), out_shape=(sds((sl...]
where the time goes in v4:
time: 51 us; the launch traced here: 50.9 us
  Pallas kernels  50.3 us (99%)
  between operations  0.64 us (1%)
    pallas_call x1, Pallas kernels, body(): pl.pallas_call(functools.partial(kernel, ctx_n, tp_n), out_shape=(sds((sl...  48 us
    pallas_call x1, Pallas kernels, body(): pl.pallas_call(functools.partial(finish, grad_scale), out_shape=(sds((sla...  2.21 us

profile of v4, /device:TPU:0, one launch (start us, length us, event | category | flops | bytes accessed | tf_op | source)
XLA Modules:
  0.0 50.9 jit_solution(2616390998016107666)
XLA Ops:
  0.6 48.0 %shard_map.110 = (bf16[192,256]{1,0:T(8,128)(2,1)}, bf16[192,256]{1,0:T(8,128)(2,1)}, bf16[192,256]{1,0:T(8,128)(2,1)}, f32[8,2,16,128]{3,2,1,0:T(8,128)}, f32[512,256]{1,0:T(8,128)}) custom-call(bf16[192,256]{1,0:T(8,128)(2,1)} %q_hbm.1, bf16[192,256]{1,0:T(8,128)(2,1)} %k_hbm.1, bf16[192,256]{1,0:T(8,128)(2,1)} %v_hbm.1, f32[256,128]{1,0:T(8,128)} %f_hbm.1, ...), custom_call_target="tpu_custom_call" | custom-call | tf_op jit(solution)/shard_map/pallas_call | solution.py:392
  48.7 2.2 %shard_map.111 = (bf16[192,256]{1,0:T(8,128)(2,1)}, bf16[192,256]{1,0:T(8,128)(2,1)}, bf16[192,256]{1,0:T(8,128)(2,1)}, f32[256,128]{1,0:T(8,128)}, f32[512,256]{1,0:T(8,128)}) custom-call(bf16[192,256]{1,0:T(8,128)(2,1)} %get-tuple-element.10.gq_ref, bf16[192,256]{1,0:T(8,128)(2,1)} %get-tuple-element.11.gk_ref, bf16[192,256]{1,0:T(8,128)(2,1)} %get-tuple-element.12.gv_ref, ...), custom_call_target="tpu_custom_call" | custom-call | tf_op jit(solution)/shard_map/pallas_call | solution.py:437
